TPU v7x, 32 devices: a whole 2x2x4 slice. The times are simulated.
32 devices in a mesh: vel: 4 (over y, x), space: 8 (over z, core).
Axes of the slice: x: 2, y: 2, z: 4, core: 2. Of those that a mesh axis runs over, the one named last changes fastest.
Arguments:
- distribution: float32 [2304, 32, 256], P('vel', 'space'), may hold values from -3 to 3
- moments_old: float32 [10, 32, 256], P(None, 'space'), may hold values from -6 to 6
- pore_mask: int32 [32, 256], P('space'), may hold values 0 or 1
- synthetic_rate: float32 [10], replicated, may hold values from 0.2 to 4
Outputs:
- distribution_new: float32 [2304, 32, 256], P('vel', 'space')
- moments_new: float32 [10, 32, 256], P(None, 'space')
Inputs may be any that keep to these rules, and one draw needn't show every extreme that they name: `pore_mask`: 1 marks a pore cell, 0 a solid one.
All inputs are finite; a program needn't handle non-finite values. No bound on the sum of `pore_mask` on one device may be relied on, other than what follows from the above.
Results may differ from a plain program's by a relative error of at most 0.000092.
Values sent between devices are 32-bit elements; how exact they have to be, the bound alone decides.
A program may use at most 64 MiB of HBM per device.

v0:
```python
import math

import jax
import jax.numpy as jnp
from jax import lax
from jax.sharding import PartitionSpec as P

VX = 16
VY = 12
VZ = 12
NY = 16
NZ = 16
TSWEEPS = 2
SWEEPS = 5


extent = 3.0
collide = 1.0
coefficients = (1.0, 2.0, 2.0, 2.0, 0.6667, 0.8, 0.8, 0.8, 2.0, 2.0)


def padded_2(cells, sides, width):
    for axis, dim in sides:
        count = lax.axis_size(axis)
        head = lax.slice_in_dim(cells, 0, width, axis=dim)
        tail = lax.slice_in_dim(cells, cells.shape[dim] - width, cells.shape[dim], axis=dim)
        cells = jnp.concatenate(
            [
                lax.ppermute(tail, axis, [(i, (i + 1) % count) for i in range(count)]),
                cells,
                lax.ppermute(head, axis, [((i + 1) % count, i) for i in range(count)]),
            ],
            axis=dim,
        )
    return cells


def node_values(indices, count):
    return -extent + (indices.astype(jnp.float32) + 0.5) * (2.0 * extent / count)


def velocity_tables(first_group, groups, along_x, along_y, along_z):
    first_nodes = node_values(first_group + jnp.arange(groups, dtype=jnp.int32), along_x)
    second_nodes = node_values(jnp.arange(along_y, dtype=jnp.int32), along_y)
    third_nodes = node_values(jnp.arange(along_z, dtype=jnp.int32), along_z)
    block_shape = (groups, along_y, along_z)
    speed_one = jnp.broadcast_to(first_nodes[:, None, None], block_shape).reshape(-1)
    speed_two = jnp.broadcast_to(second_nodes[None, :, None], block_shape).reshape(-1)
    speed_three = jnp.broadcast_to(third_nodes[None, None, :], block_shape).reshape(-1)
    energy = speed_one * speed_one + speed_two * speed_two + speed_three * speed_three
    functions = jnp.stack(
        [
            jnp.ones_like(energy),
            speed_one,
            speed_two,
            speed_three,
            energy - 1.5,
            speed_one * (energy - 2.5),
            speed_two * (energy - 2.5),
            speed_three * (energy - 2.5),
            speed_one * speed_two,
            speed_two * speed_three,
        ]
    )
    volume = (2.0 * extent) ** 3 / (along_x * along_y * along_z) / math.pi**1.5
    moment_rows = functions * volume
    factors = jnp.array(coefficients, dtype=jnp.float32)
    spread_rows = jnp.transpose(functions * factors[:, None] * jnp.exp(-energy)[None, :])
    return ((speed_one, speed_two, speed_three), moment_rows, spread_rows)


def upwind_sweep(padded, source, porous, speeds, along_y, along_z):
    speed_one, speed_two, speed_three = speeds
    middle = padded[:, 1:-1]
    groups, thickness, plane_cells = middle.shape
    cube_view = middle.reshape(groups, thickness, along_y, along_z)
    from_first = jnp.where(speed_one[:, None, None] > 0, padded[:, :-2], padded[:, 2:])
    from_second = jnp.where(
        speed_two[:, None, None, None] > 0, jnp.roll(cube_view, 1, 2), jnp.roll(cube_view, -1, 2)
    )
    from_third = jnp.where(
        speed_three[:, None, None, None] > 0, jnp.roll(cube_view, 1, 3), jnp.roll(cube_view, -1, 3)
    )
    across = (
        jnp.abs(speed_two)[:, None, None, None] * from_second
        + jnp.abs(speed_three)[:, None, None, None] * from_third
    )
    inflow = jnp.abs(speed_one)[:, None, None] * from_first + across.reshape(
        groups, thickness, plane_cells
    )
    denominator = collide + jnp.abs(speed_one) + jnp.abs(speed_two) + jnp.abs(speed_three)
    return porous[None] * (collide * source + inflow) / denominator[:, None, None]


def relax_step(padded, forcing, porous, rates, along_y, along_z):
    middle = padded[:, 1:-1]
    moment_count, thickness, plane_cells = middle.shape
    cube_view = middle.reshape(moment_count, thickness, along_y, along_z)
    beside = (
        jnp.roll(cube_view, 1, 2)
        + jnp.roll(cube_view, -1, 2)
        + jnp.roll(cube_view, 1, 3)
        + jnp.roll(cube_view, -1, 3)
    )
    neighbours = (
        padded[:, :-2] + padded[:, 2:] + beside.reshape(moment_count, thickness, plane_cells)
    )
    return porous[None] * (forcing + neighbours) / (rates + 6.0)[:, None, None]


def lift(spread_rows, fields):
    moment_count = fields.shape[0]
    flat = jnp.dot(
        spread_rows,
        fields.reshape(moment_count, -1),
        precision=lax.Precision.HIGHEST,
        preferred_element_type=jnp.float32,
    )
    return flat.reshape(spread_rows.shape[0], fields.shape[1], fields.shape[2])


def body(distribution, moments_old, pore_mask, synthetic_rate):
    porous = pore_mask.astype(jnp.float32)
    velocities, thickness, plane_cells = distribution.shape
    moment_count = moments_old.shape[0]
    local_groups = velocities // (VY * VZ)
    first_group = lax.axis_index("vel") * local_groups
    speeds, moment_rows, spread_rows = velocity_tables(first_group, local_groups, VX, VY, VZ)
    source = lift(spread_rows, moments_old)
    current = distribution
    for sweep_number in range(TSWEEPS):
        padded = padded_2(current, (("space", 1),), 1)
        current = upwind_sweep(padded, source, porous, speeds, NY, NZ)
    partial_value = jnp.dot(
        moment_rows,
        current.reshape(velocities, -1),
        precision=lax.Precision.HIGHEST,
        preferred_element_type=jnp.float32,
    ).reshape(moment_count, thickness, plane_cells)
    moments_half = lax.psum(partial_value, "vel")
    change = moments_half - moments_old
    denominators = (synthetic_rate + 6.0)[:, None, None]
    correction = porous[None] * change / denominators
    for sweep_number in range(SWEEPS - 1):
        padded = padded_2(correction, (("space", 1),), 1)
        correction = relax_step(padded, change, porous, synthetic_rate, NY, NZ)
    moments_new = moments_half + correction
    distribution_new = current + porous[None] * lift(spread_rows, correction)
    return (distribution_new, moments_new)


def solution(mesh):
    placed = (P("vel", "space", None), P(None, "space", None), P("space", None), P())
    return jax.shard_map(
        body,
        mesh=mesh,
        in_specs=placed,
        out_specs=(P("vel", "space", None), P(None, "space", None)),
        check_vma=False,
    )
```

profile of v0, /device:TPU:0, one launch (start us, length us, event | category | flops | bytes accessed | tf_op | source)
XLA Modules:
  0.0 139.6 jit_solution(11379801926522163604)
XLA Ops:
  0.6 2.1 %copy.23 = f32[576,4,256]{2,0,1:T(8,128)S(1)} copy(f32[576,4,256]{2,1,0:T(4,128)} %param.5) | data formatting | bytes 4718592 | tf_op args[0]
  2.8 1.2 fusion.74
  3.9 0.5 collective-permute-start
  4.4 4.0 %collective-permute-start.1 = (f32[576,1,256]{2,0,1:T(8,128)}, f32[576,1,256]{2,0,1:T(8,128)}, u32[]{:S(2)}, u32[]{:S(2)}) collective-permute-start(f32[576,1,256]{2,0,1:T(8,128)} %get-tuple-element.31), channel_id=1, source_target_pairs={{1,0},{2,1},{3,2},{4,3},{5,4},{6,5},{7,6},{0,7},{9,8},{10,9},{11,1... | collective-permute-start | bytes 1769480 | tf_op jit(solution)/shard_map/ppermute | solution.py:31
  8.4 3.0 %copy.27 = f32[576,4,256]{0,2,1:T(8,128)S(1)} copy(f32[576,4,256]{2,1,0:T(4,128)} %param.5) | data formatting | bytes 4718592 | tf_op args[0]
  11.5 2.6 %fusion.69 = (f32[576,4,15,16]{0,3,2,1:T(8,128)}, f32[576,4,15,16]{0,3,2,1:T(8,128)}) fusion(f32[576,4,16,16]{0,3,2,1:T(8,128)S(1)} %bitcast.61), kind=kLoop, calls=%fused_computation.106 | loop fusion | bytes 8847360 | tf_op jit(solution)/shard_map/jit(_roll_static)/slice | solution.py:79
  14.1 2.7 %fusion.71 = (f32[576,4,16,15]{0,3,2,1:T(8,128)}, f32[576,4,16,15]{0,3,2,1:T(8,128)}) fusion(f32[576,4,16,16]{0,3,2,1:T(8,128)S(1)} %bitcast.63), kind=kLoop, calls=%fused_computation.108 | loop fusion | bytes 8847360 | tf_op jit(solution)/shard_map/jit(_roll_static)/slice | solution.py:82
  16.8 0.2 fusion.72
  17.6 4.4 %pad_maximum_fusion = (f32[576,4,16,16]{0,3,2,1:T(8,128)}, f32[576,4,16,16]{0,3,2,1:T(8,128)S(1)}) fusion(f32[576,4,15,16]{0,3,2,1:T(8,128)} %get-tuple-element.21, f32[576,4,1,16]{0,3,2,1:T(8,128)S(1)} %get-tuple-element.23, f32[576,4,1,16]{0,3,2,1:T(8,128)S(1)} %get-tuple-element.22, f32[576,4,15,16]{0,3,2,1:T(8,128)} %get-tuple-element.20), kind=kLoop, calls=%fused_computation | loop fusion | flops 1179648 | bytes 9437184 | tf_op jit(solution)/shard_map/jit(_roll_static)/concatenate | solution.py:79
  22.0 3.2 %copy.28 = f32[576,4,256]{2,0,1:T(8,128)} copy(f32[576,4,256]{0,2,1:T(8,128)} %bitcast.66) | data formatting | bytes 4718592 | tf_op jit(solution)/shard_map/jit(_roll_static)/concatenate | solution.py:79
  25.2 2.0 %copy.29 = f32[576,4,256]{2,0,1:T(8,128)} copy(f32[576,4,256]{0,2,1:T(8,128)S(1)} %bitcast.65) | data formatting | bytes 4718592 | tf_op jit(solution)/shard_map/jit(_roll_static)/concatenate | solution.py:79
  27.2 4.7 %pad_maximum_fusion.2 = (f32[576,4,16,16]{0,3,2,1:T(8,128)}, f32[576,4,16,16]{0,3,2,1:T(8,128)S(1)}) fusion(f32[576,4,16,15]{0,3,2,1:T(8,128)} %get-tuple-element.25, f32[576,4,16,1]{0,3,2,1:T(1,128)S(1)} %get-tuple-element.27, f32[576,4,16,1]{0,3,2,1:T(1,128)S(1)} %get-tuple-element.26, f32[576,4,16,15]{0,3,2,1:T(8,128)} %get-tuple-element.24), kind=kLoop, calls=%fused_computation.2 | loop fusion | flops 1179648 | bytes 9437184 | tf_op jit(solution)/shard_map/jit(_roll_static)/concatenate | solution.py:82
  31.9 3.1 %copy.30 = f32[576,4,256]{2,0,1:T(8,128)} copy(f32[576,4,256]{0,2,1:T(8,128)} %bitcast.72) | data formatting | bytes 4718592 | tf_op jit(solution)/shard_map/jit(_roll_static)/concatenate | solution.py:82
  35.1 2.0 %copy.31 = f32[576,4,256]{2,0,1:T(8,128)} copy(f32[576,4,256]{0,2,1:T(8,128)S(1)} %bitcast.71) | data formatting | bytes 4718592 | tf_op jit(solution)/shard_map/jit(_roll_static)/concatenate | solution.py:82
  38.5 10.3 %fusion.14 = (f32[576,4,256]{2,0,1:T(8,128)}, f32[576,4,256]{2,0,1:T(8,128)}) fusion(f32[576,1,256]{2,0,1:T(8,128)} %collective-permute-done.1, f32[576,4,256]{2,0,1:T(8,128)} %copy-done.2, f32[576,1,256]{2,0,1:T(8,128)} %collective-permute-done, f32[576,4,256]{2,0,1:T(8,128)} %copy.30, f32[576,4,256]{2,0,1:T(8,128)} %copy.31, f32[576,4,256]{2,0,1:T(8,128)} %copy.28, ...), kind=kOutput, calls=%fused_computation.25 | convolution fusion | flops 78458112 | bytes 17776104 | tf_op jit(solution)/shard_map/dot_general | solution.py:113
  48.9 2.1 %copy.32 = f32[576,4,256]{0,2,1:T(8,128)S(1)} copy(f32[576,4,256]{2,0,1:T(8,128)} %get-tuple-element.77) | data formatting | bytes 4718592 | tf_op jit(solution)/shard_map/div | solution.py:92
  51.0 1.9 %fusion.65 = (f32[576,4,15,16]{0,3,2,1:T(8,128)S(1)}, f32[576,4,15,16]{0,3,2,1:T(8,128)}) fusion(f32[576,4,16,16]{0,3,2,1:T(8,128)S(1)} %bitcast.57), kind=kLoop, calls=%fused_computation.102 | loop fusion | bytes 8847360 | tf_op jit(solution)/shard_map/jit(_roll_static)/slice | solution.py:79
  52.9 2.6 %fusion.67 = (f32[576,4,16,15]{0,3,2,1:T(8,128)}, f32[576,4,16,15]{0,3,2,1:T(8,128)}) fusion(f32[576,4,16,16]{0,3,2,1:T(8,128)S(1)} %bitcast.59), kind=kLoop, calls=%fused_computation.104 | loop fusion | bytes 8847360 | tf_op jit(solution)/shard_map/jit(_roll_static)/slice | solution.py:82
  55.5 1.2 fusion.73
  56.7 1.7 %pad_maximum_fusion.5 = f32[576,4,16,16]{0,3,2,1:T(8,128)} fusion(f32[576,4,1,16]{0,3,2,1:T(8,128)S(1)} %get-tuple-element.14, f32[576,4,15,16]{0,3,2,1:T(8,128)S(1)} %get-tuple-element.12), kind=kLoop, calls=%fused_computation.5 | loop fusion | flops 589824 | bytes 4718592 | tf_op jit(solution)/shard_map/jit(_roll_static)/concatenate | solution.py:79
  58.4 3.1 %copy.34 = f32[576,4,256]{2,0,1:T(8,128)} copy(f32[576,4,256]{0,2,1:T(8,128)} %bitcast.67) | data formatting | bytes 4718592 | tf_op jit(solution)/shard_map/jit(_roll_static)/concatenate | solution.py:79
  61.5 3.4 %pad_maximum_fusion.4 = f32[576,4,16,16]{0,3,2,1:T(8,128)} fusion(f32[576,4,15,16]{0,3,2,1:T(8,128)} %get-tuple-element.13, f32[576,4,1,16]{0,3,2,1:T(8,128)S(1)} %get-tuple-element.15), kind=kLoop, calls=%fused_computation.4 | loop fusion | flops 589824 | bytes 4718592 | tf_op jit(solution)/shard_map/jit(_roll_static)/concatenate | solution.py:79
  64.9 3.2 %copy.33 = f32[576,4,256]{2,0,1:T(8,128)} copy(f32[576,4,256]{0,2,1:T(8,128)} %bitcast.68) | data formatting | bytes 4718592 | tf_op jit(solution)/shard_map/jit(_roll_static)/concatenate | solution.py:79
  68.1 3.5 %collective-permute-start.3 = (f32[576,1,256]{2,0,1:T(8,128)}, f32[576,1,256]{2,0,1:T(8,128)}, u32[]{:S(2)}, u32[]{:S(2)}) collective-permute-start(f32[576,1,256]{2,0,1:T(8,128)} %get-tuple-element.29), channel_id=1, source_target_pairs={{1,0},{2,1},{3,2},{4,3},{5,4},{6,5},{7,6},{0,7},{9,8},{10,9},{11,1... | collective-permute-start | bytes 1769480 | tf_op jit(solution)/shard_map/ppermute | solution.py:31
  71.7 0.2 fusion.68
  71.9 3.6 %pad_maximum_fusion.7 = f32[576,4,16,16]{0,3,2,1:T(8,128)} fusion(f32[576,4,16,1]{0,3,2,1:T(1,128)S(1)} %get-tuple-element.18, f32[576,4,16,15]{0,3,2,1:T(8,128)} %get-tuple-element.16), kind=kLoop, calls=%fused_computation.7 | loop fusion | flops 589824 | bytes 4718592 | tf_op jit(solution)/shard_map/jit(_roll_static)/concatenate | solution.py:82
  75.5 3.3 %copy.36 = f32[576,4,256]{2,0,1:T(8,128)} copy(f32[576,4,256]{0,2,1:T(8,128)} %bitcast.69) | data formatting | bytes 4718592 | tf_op jit(solution)/shard_map/jit(_roll_static)/concatenate | solution.py:82
  78.8 1.8 %pad_maximum_fusion.6 = f32[576,4,16,16]{0,3,2,1:T(8,128)} fusion(f32[576,4,16,15]{0,3,2,1:T(8,128)S(1)} %copy-done.1, f32[576,4,16,1]{0,3,2,1:T(1,128)S(1)} %get-tuple-element.19), kind=kLoop, calls=%fused_computation.6 | loop fusion | flops 589824 | bytes 4718592 | tf_op jit(solution)/shard_map/jit(_roll_static)/concatenate | solution.py:82
  80.6 3.1 %copy.35 = f32[576,4,256]{2,0,1:T(8,128)} copy(f32[576,4,256]{0,2,1:T(8,128)} %bitcast.70) | data formatting | bytes 4718592 | tf_op jit(solution)/shard_map/jit(_roll_static)/concatenate | solution.py:82
  83.7 1.2 collective-permute-done.2
  85.0 6.3 %fusion.8 = f32[576,4,256]{2,0,1:T(8,128)S(1)} fusion(f32[576,4,256]{2,0,1:T(8,128)} %get-tuple-element.78, f32[576,1,256]{2,0,1:T(8,128)} %collective-permute-done.3, f32[576,4,256]{2,0,1:T(8,128)} %get-tuple-element.77, f32[576,1,256]{2,0,1:T(8,128)S(1)} %collective-permute-done.2, f32[576,4,256]{2,0,1:T(8,128)} %copy.35, f32[576,4,256]{2,0,1:T(8,128)} %copy.36, ...), kind=kLoop, calls=%fused_computation.17 | loop fusion | flops 7667712 | bytes 17709760 | tf_op jit(solution)/shard_map/div | solution.py:92
  91.3 1.3 fusion
  92.6 17.9 %psum.7 = f32[10,4,256]{2,0,1:T(8,128)S(1)} all-reduce(f32[10,4,256]{2,0,1:T(8,128)S(1)} %fusion), channel_id=1, replica_groups=mesh['vel'=4,'space'=8] {'vel'}, use_global_device_ids=true, to_apply=%region_0.1 | all-reduce | flops 10240 | bytes 81920 | tf_op jit(solution)/shard_map/psum | solution.py:140
  111.2 3.5 %collective-permute-start.5 = (f32[10,1,256]{2,0,1:T(8,128)S(1)}, f32[10,1,256]{2,0,1:T(8,128)S(1)}, u32[]{:S(2)}, u32[]{:S(2)}) collective-permute-start(f32[10,1,256]{2,0,1:T(8,128)S(1)} %get-tuple-element.71), channel_id=1, source_target_pairs={{1,0},{2,1},{3,2},{4,3},{5,4},{6,5},{7,6},{0,7},{9,8},{10,9},{11,1... | collective-permute-start | bytes 30728 | tf_op jit(solution)/shard_map/ppermute | solution.py:31
  114.8 0.3 fusion.16
  115.2 1.0 collective-permute-done.4
  117.0 3.6 %collective-permute-start.7 = (f32[10,1,256]{2,0,1:T(8,128)S(1)}, f32[10,1,256]{2,0,1:T(8,128)S(1)}, u32[]{:S(2)}, u32[]{:S(2)}) collective-permute-start(f32[10,1,256]{2,0,1:T(8,128)S(1)} %get-tuple-element.69), channel_id=1, source_target_pairs={{1,0},{2,1},{3,2},{4,3},{5,4},{6,5},{7,6},{0,7},{9,8},{10,9},{11,1... | collective-permute-start | bytes 30728 | tf_op jit(solution)/shard_map/ppermute | solution.py:31
  120.6 0.3 fusion.18
  121.0 0.9 collective-permute-done.6
  122.8 3.6 %collective-permute-start.9 = (f32[10,1,256]{2,0,1:T(8,128)S(1)}, f32[10,1,256]{2,0,1:T(8,128)S(1)}, u32[]{:S(2)}, u32[]{:S(2)}) collective-permute-start(f32[10,1,256]{2,0,1:T(8,128)S(1)} %get-tuple-element.67), channel_id=1, source_target_pairs={{1,0},{2,1},{3,2},{4,3},{5,4},{6,5},{7,6},{0,7},{9,8},{10,9},{11,1... | collective-permute-start | bytes 30728 | tf_op jit(solution)/shard_map/ppermute | solution.py:31
  126.4 0.3 fusion.20
  126.8 0.9 collective-permute-done.8
  128.6 3.6 %collective-permute-start.11 = (f32[10,1,256]{2,0,1:T(8,128)S(1)}, f32[10,1,256]{2,0,1:T(8,128)S(1)}, u32[]{:S(2)}, u32[]{:S(2)}) collective-permute-start(f32[10,1,256]{2,0,1:T(8,128)S(1)} %get-tuple-element.65), channel_id=1, source_target_pairs={{1,0},{2,1},{3,2},{4,3},{5,4},{6,5},{7,6},{0,7},{9,8},{10,9},{11,1... | collective-permute-start | bytes 30728 | tf_op jit(solution)/shard_map/ppermute | solution.py:31
  132.1 0.3 fusion.22
  132.6 0.9 collective-permute-done.10
  133.8 2.2 %multiply_add_fusion = f32[576,4,256]{2,0,1:T(8,128)S(1)} fusion(f32[576,4,256]{2,0,1:T(8,128)S(1)} %fusion.8, f32[4,256]{1,0:T(4,128)S(1)} %convert_element_type.60, f32[4,256,10]{1,0,2:T(4,128)S(1)} %dot_general.28, f32[10,576]{1,0:T(8,128)S(1)} %stack.2, f32[576]{0:T(1024)S(1)} %reshape.333, f32[10]{0:T(128)S(1)} %copy-done.5), kind=kOutput, calls=%fused_computation.27 | convolution fusion | flops 71970048 | bytes 4789032 | tf_op jit(solution)/shard_map/dot_general | solution.py:113
  136.0 2.9 %copy.50 = f32[576,4,256]{2,1,0:T(4,128)} copy(f32[576,4,256]{2,0,1:T(8,128)S(1)} %multiply_add_fusion) | data formatting | bytes 4718592
  139.0 0.6 copy.51
  (106 shorter events, 5.9 us)
Async XLA Ops:
  2.8 5.7 %copy-start.2 = (f32[576,4,256]{2,0,1:T(8,128)}, f32[576,4,256]{2,0,1:T(8,128)S(1)}, u32[]{:S(2)}) copy-start(f32[576,4,256]{2,0,1:T(8,128)S(1)} %copy.23) | copy-start | bytes 7077892
  3.9 34.6 %collective-permute-start = (f32[576,1,256]{2,0,1:T(8,128)}, f32[576,1,256]{2,0,1:T(8,128)}, u32[]{:S(2)}, u32[]{:S(2)}) collective-permute-start(f32[576,1,256]{2,0,1:T(8,128)} %get-tuple-element.30), channel_id=1, source_target_pairs={{0,1},{1,2},{2,3},{3,4},{4,5},{5,6},{6,7},{7,0},{8,9},{9,10},{10,1... | collective-permute-start | bytes 1769480 | tf_op jit(solution)/shard_map/ppermute | solution.py:29
  4.4 34.1 %collective-permute-start.1 = (f32[576,1,256]{2,0,1:T(8,128)}, f32[576,1,256]{2,0,1:T(8,128)}, u32[]{:S(2)}, u32[]{:S(2)}) collective-permute-start(f32[576,1,256]{2,0,1:T(8,128)} %get-tuple-element.31), channel_id=1, source_target_pairs={{1,0},{2,1},{3,2},{4,3},{5,4},{6,5},{7,6},{0,7},{9,8},{10,9},{11,1... | collective-permute-start | bytes 1769480 | tf_op jit(solution)/shard_map/ppermute | solution.py:31
  35.0 2.5 %copy-start.4 = (s32[4,256]{1,0:T(4,128)S(1)}, s32[4,256]{1,0:T(4,128)}, u32[]{:S(2)}) copy-start(s32[4,256]{1,0:T(4,128)} %param.7) | copy-start | bytes 12292
  35.0 3.2 %copy-start.3 = (f32[10,4,256]{2,1,0:T(4,128)S(1)}, f32[10,4,256]{2,1,0:T(4,128)}, u32[]{:S(2)}) copy-start(f32[10,4,256]{2,1,0:T(4,128)} %param.6) | copy-start | bytes 122884
  35.0 3.4 %copy-start.6 = (f32[10]{0:T(128)S(1)}, f32[10]{0:T(128)}, u32[]{:S(2)}) copy-start(f32[10]{0:T(128)} %param.8) | copy-start | bytes 124
  35.0 3.5 %copy-start.5 = (f32[10]{0:T(128)S(1)}, f32[10]{0:T(128)}, u32[]{:S(2)}) copy-start(f32[10]{0:T(128)} %constant.11.clone) | copy-start | bytes 124
  52.9 2.6 %copy-start = (f32[576,4,256]{2,0,1:T(8,128)S(1)}, f32[576,4,256]{2,0,1:T(8,128)}, u32[]{:S(2)}) copy-start(f32[576,4,256]{2,0,1:T(8,128)} %get-tuple-element.77) | copy-start | bytes 7077892
  68.1 16.9 %collective-permute-start.2 = (f32[576,1,256]{2,0,1:T(8,128)}, f32[576,1,256]{2,0,1:T(8,128)S(1)}, u32[]{:S(2)}, u32[]{:S(2)}) collective-permute-start(f32[576,1,256]{2,0,1:T(8,128)} %get-tuple-element.28), channel_id=1, source_target_pairs={{0,1},{1,2},{2,3},{3,4},{4,5},{5,6},{6,7},{7,0},{8,9},{9,10},{10,1... | collective-permute-start | bytes 1769480 | tf_op jit(solution)/shard_map/ppermute | solution.py:29
  68.1 16.9 %collective-permute-start.3 = (f32[576,1,256]{2,0,1:T(8,128)}, f32[576,1,256]{2,0,1:T(8,128)}, u32[]{:S(2)}, u32[]{:S(2)}) collective-permute-start(f32[576,1,256]{2,0,1:T(8,128)} %get-tuple-element.29), channel_id=1, source_target_pairs={{1,0},{2,1},{3,2},{4,3},{5,4},{6,5},{7,6},{0,7},{9,8},{10,9},{11,1... | collective-permute-start | bytes 1769480 | tf_op jit(solution)/shard_map/ppermute | solution.py:31
  75.5 3.3 %copy-start.1 = (f32[576,4,16,15]{0,3,2,1:T(8,128)S(1)}, f32[576,4,16,15]{0,3,2,1:T(8,128)}, u32[]{:S(2)}) copy-start(f32[576,4,16,15]{0,3,2,1:T(8,128)} %get-tuple-element.17) | copy-start | bytes 6635524
  111.2 5.0 %collective-permute-start.4 = (f32[10,1,256]{2,0,1:T(8,128)S(1)}, f32[10,1,256]{2,0,1:T(8,128)S(1)}, u32[]{:S(2)}, u32[]{:S(2)}) collective-permute-start(f32[10,1,256]{2,0,1:T(8,128)S(1)} %get-tuple-element.70), channel_id=1, source_target_pairs={{0,1},{1,2},{2,3},{3,4},{4,5},{5,6},{6,7},{7,0},{8,9},{9,10},{10,1... | collective-permute-start | bytes 30728 | tf_op jit(solution)/shard_map/ppermute | solution.py:29
  111.2 5.0 %collective-permute-start.5 = (f32[10,1,256]{2,0,1:T(8,128)S(1)}, f32[10,1,256]{2,0,1:T(8,128)S(1)}, u32[]{:S(2)}, u32[]{:S(2)}) collective-permute-start(f32[10,1,256]{2,0,1:T(8,128)S(1)} %get-tuple-element.71), channel_id=1, source_target_pairs={{1,0},{2,1},{3,2},{4,3},{5,4},{6,5},{7,6},{0,7},{9,8},{10,9},{11,1... | collective-permute-start | bytes 30728 | tf_op jit(solution)/shard_map/ppermute | solution.py:31
  116.9 5.0 %collective-permute-start.6 = (f32[10,1,256]{2,0,1:T(8,128)S(1)}, f32[10,1,256]{2,0,1:T(8,128)S(1)}, u32[]{:S(2)}, u32[]{:S(2)}) collective-permute-start(f32[10,1,256]{2,0,1:T(8,128)S(1)} %get-tuple-element.68), channel_id=1, source_target_pairs={{0,1},{1,2},{2,3},{3,4},{4,5},{5,6},{6,7},{7,0},{8,9},{9,10},{10,1... | collective-permute-start | bytes 30728 | tf_op jit(solution)/shard_map/ppermute | solution.py:29
  117.0 5.0 %collective-permute-start.7 = (f32[10,1,256]{2,0,1:T(8,128)S(1)}, f32[10,1,256]{2,0,1:T(8,128)S(1)}, u32[]{:S(2)}, u32[]{:S(2)}) collective-permute-start(f32[10,1,256]{2,0,1:T(8,128)S(1)} %get-tuple-element.69), channel_id=1, source_target_pairs={{1,0},{2,1},{3,2},{4,3},{5,4},{6,5},{7,6},{0,7},{9,8},{10,9},{11,1... | collective-permute-start | bytes 30728 | tf_op jit(solution)/shard_map/ppermute | solution.py:31
  122.7 5.0 %collective-permute-start.8 = (f32[10,1,256]{2,0,1:T(8,128)S(1)}, f32[10,1,256]{2,0,1:T(8,128)S(1)}, u32[]{:S(2)}, u32[]{:S(2)}) collective-permute-start(f32[10,1,256]{2,0,1:T(8,128)S(1)} %get-tuple-element.66), channel_id=1, source_target_pairs={{0,1},{1,2},{2,3},{3,4},{4,5},{5,6},{6,7},{7,0},{8,9},{9,10},{10,1... | collective-permute-start | bytes 30728 | tf_op jit(solution)/shard_map/ppermute | solution.py:29
  122.8 5.0 %collective-permute-start.9 = (f32[10,1,256]{2,0,1:T(8,128)S(1)}, f32[10,1,256]{2,0,1:T(8,128)S(1)}, u32[]{:S(2)}, u32[]{:S(2)}) collective-permute-start(f32[10,1,256]{2,0,1:T(8,128)S(1)} %get-tuple-element.67), channel_id=1, source_target_pairs={{1,0},{2,1},{3,2},{4,3},{5,4},{6,5},{7,6},{0,7},{9,8},{10,9},{11,1... | collective-permute-start | bytes 30728 | tf_op jit(solution)/shard_map/ppermute | solution.py:31
  128.5 5.0 %collective-permute-start.10 = (f32[10,1,256]{2,0,1:T(8,128)S(1)}, f32[10,1,256]{2,0,1:T(8,128)S(1)}, u32[]{:S(2)}, u32[]{:S(2)}) collective-permute-start(f32[10,1,256]{2,0,1:T(8,128)S(1)} %get-tuple-element.64), channel_id=1, source_target_pairs={{0,1},{1,2},{2,3},{3,4},{4,5},{5,6},{6,7},{7,0},{8,9},{9,10},{10,1... | collective-permute-start | bytes 30728 | tf_op jit(solution)/shard_map/ppermute | solution.py:29
  128.6 5.0 %collective-permute-start.11 = (f32[10,1,256]{2,0,1:T(8,128)S(1)}, f32[10,1,256]{2,0,1:T(8,128)S(1)}, u32[]{:S(2)}, u32[]{:S(2)}) collective-permute-start(f32[10,1,256]{2,0,1:T(8,128)S(1)} %get-tuple-element.65), channel_id=1, source_target_pairs={{1,0},{2,1},{3,2},{4,3},{5,4},{6,5},{7,6},{0,7},{9,8},{10,9},{11,1... | collective-permute-start | bytes 30728 | tf_op jit(solution)/shard_map/ppermute | solution.py:31
where the time goes:
time: 140 us
  local copies, waits for them, and re-layouts  51.4 us (37%)
  other arithmetic  27.6 us (20%)
  starting transfers between devices  22.5 us (16%)
  blocking collectives  17.9 us (13%)
  matrix products  13.8 us (10%)
  waiting for transfers between devices  5.17 us (4%)
    ppermute x6, starting transfers between devices, padded_2(): lax.ppermute(head, axis, [((i + 1) % count, i) for i in range(count)])  21.8 us
    psum x1, blocking collectives, body(): moments_half = lax.psum(partial_value, 'vel')  17.9 us
    dot_general x2, matrix products, lift(): jnp.dot(spread_rows, fields.reshape(moment_count, -1), precision=lax.Prec...  12.6 us
    unnamed x22, local copies, waits for them, and re-layouts  8.79 us
    concatenate x2, other arithmetic, upwind_sweep(): jnp.roll(cube_view, 1, 2)  7.8 us
    concatenate x2, other arithmetic, upwind_sweep(): jnp.roll(cube_view, 1, 3)  6.52 us
    concatenate x2, local copies, waits for them, and re-layouts, upwind_sweep(): jnp.roll(cube_view, 1, 2)  6.39 us
    div x1, other arithmetic, upwind_sweep(): porous[None] * (collide * source + inflow) / denominator[:, None, None]  6.31 us
  transfers between devices with their start and end apart: 12, of which 8 were waited for; matrix products, arithmetic and copies ran while one was open for 31% of the time, Pallas kernels for 0%

commit v1 on v0

v1 whole, which is shorter than its diff:
```python
import functools
import math

import jax
import jax.numpy as jnp
from jax import lax
from jax.experimental import pallas as pl
from jax.experimental.pallas import tpu as pltpu
from jax.sharding import PartitionSpec as P

VX = 16
VY = 12
VZ = 12
NY = 16
NZ = 16
TSWEEPS = 2
SWEEPS = 5

extent = 3.0
coefficients = (1.0, 2.0, 2.0, 2.0, 0.6667, 0.8, 0.8, 0.8, 2.0, 2.0)
NMOM = len(coefficients)
LANES = 128
ROWS = 8
HALF = VY // 2
CHUNK = HALF * VZ
MESH = pl.DeviceIdType.MESH


def node(index, count):
    return -extent + (index.astype(jnp.float32) + 0.5) * (2.0 * extent / count)


def node_c(k):
    return -extent + (k + 0.5) * (2.0 * extent / VZ)


def poly_parts(fields, a, b):
    k = coefficients
    q = a * a + b * b
    m = fields
    p2 = k[4] * m[4] + (k[5] * a) * m[5] + (k[6] * b) * m[6]
    p0 = (
        k[0] * m[0]
        + (k[1] * a) * m[1]
        + (k[2] * b) * m[2]
        + (k[4] * (q - 1.5)) * m[4]
        + (k[5] * a * (q - 2.5)) * m[5]
        + (k[6] * b * (q - 2.5)) * m[6]
        + (k[8] * a * b) * m[8]
    )
    p1 = k[3] * m[3] + (k[7] * (q - 2.5)) * m[7] + (k[9] * b) * m[9]
    p3 = k[7] * m[7]
    weight = jnp.exp(jnp.full((ROWS, LANES), -q, jnp.float32))
    return weight * p0, weight * p1, weight * p2, weight * p3


def poly_pair(parts, c):
    p0, p1, p2, p3 = parts
    g = math.exp(-c * c)
    even = g * p0 + (g * c * c) * p2
    odd = (g * c) * p1 + (g * c * c * c) * p3
    return even - odd, even + odd


def masks():
    lane = lax.broadcasted_iota(jnp.int32, (ROWS, LANES), 1)
    row = lax.broadcasted_iota(jnp.int32, (ROWS, LANES), 0)
    return lane, row


def from_y(f, step, lane):
    turned = pltpu.roll(f, (step * NZ) % LANES, 1)
    other = pltpu.roll(turned, ROWS // 2, 0)
    inside = (lane >= NZ) if step > 0 else (lane < LANES - NZ)
    return jnp.where(inside, turned, other)


def from_z(f, step, lane):
    near = pltpu.roll(f, step % LANES, 1)
    wrapped = pltpu.roll(f, (-step * (NZ - 1)) % LANES, 1)
    inside = (lane % NZ != 0) if step > 0 else (lane % NZ != NZ - 1)
    return jnp.where(inside, near, wrapped)


def transport_kernel(
    nvel, nspace, groups,
    f_hbm, m_ref, pore_ref, rate_ref,
    half_hbm, mnew_ref, corr_ref,
    f_ref, h_ref, g_ref, fsend, hsend, frecv, hrecv,
    acc, mrecv, pore_ext, change_ext,
    in_sem, out_sem, fs_sem, fr_sem, hs_sem, hr_sem, ms_sem, mr_sem, ps_sem, pr_sem, cs_sem, cr_sem,
):
    vel = lax.axis_index("vel")
    space = lax.axis_index("space")
    right = lax.rem(space + 1, nspace)
    left = lax.rem(space + nspace - 1, nspace)
    chunks = groups * 2
    positive = vel * 2 >= nvel
    target = jnp.where(positive, right, left)
    volume = (2.0 * extent) ** 3 / (VX * VY * VZ) / math.pi**1.5

    def load(c):
        rows = pl.ds(c * (CHUNK * ROWS), CHUNK * ROWS)
        return pltpu.make_async_copy(f_hbm.at[rows], f_ref.at[rows], in_sem.at[c])

    for c in range(chunks):
        load(c).start()

    barrier = pltpu.get_barrier_semaphore()
    for other in (left, right):
        pl.semaphore_signal(barrier, inc=1, device_id={"space": other}, device_id_type=MESH)
    for d in range(1, nvel):
        pl.semaphore_signal(
            barrier, inc=1, device_id={"vel": lax.rem(vel + d, nvel)}, device_id_type=MESH
        )

    lane, row = masks()
    plane = lax.rem(row, ROWS // 2)
    pore = pore_ref[...].astype(jnp.float32)
    pore_ext[1] = pore
    edge = jnp.where(positive, 0, ROWS // 2 - 1)
    at_edge = jnp.where(plane == edge, 1.0, 0.0)
    off_edge = 1.0 - at_edge
    acc[...] = jnp.zeros_like(acc)
    fields = [m_ref[pl.ds(m * ROWS, ROWS), :] for m in range(NMOM)]

    def upwind_x(f):
        return jnp.where(positive, pltpu.roll(f, 1, 0), pltpu.roll(f, ROWS - 1, 0))

    def pack(src, base):
        lastp = src[pl.ds(base + ROWS // 2 - 1, ROWS, stride=ROWS // 2), :]
        firstp = src[pl.ds(base, ROWS, stride=ROWS // 2), :]
        return jnp.where(positive, lastp, firstp)

    def pack_chunk(src, dst, c):
        for t in range(CHUNK // 4):
            base = pl.multiple_of(c * (CHUNK * ROWS), ROWS) + t * 4 * ROWS
            dst[pl.ds(pl.multiple_of(c * (CHUNK * 2), ROWS) + t * ROWS, ROWS), :] = pack(src, base)

    def send(src, dst, s_sem, r_sem, c):
        rows = pl.ds(c * (CHUNK * 2), CHUNK * 2)
        return pltpu.make_async_remote_copy(
            src_ref=src.at[rows], dst_ref=dst.at[rows],
            send_sem=s_sem.at[c], recv_sem=r_sem.at[c],
            device_id={"space": target}, device_id_type=MESH,
        )

    def edges(src, dst, s_sem, r_sem):
        return [
            pltpu.make_async_remote_copy(
                src_ref=src.at[1], dst_ref=dst.at[2 * (1 - s)],
                send_sem=s_sem.at[s], recv_sem=r_sem.at[s],
                device_id={"space": (left, right)[s]}, device_id_type=MESH,
            )
            for s in range(2)
        ]

    def sweep(f, src, w, amask, ab, ac, bstep, cstep):
        total = src + amask * upwind_x(f)
        total = total + ab * from_y(f, bstep, lane)
        total = total + ac * from_z(f, cstep, lane)
        return w * total

    def node_ab(group, half, jj):
        a = node(vel * groups + group, VX)
        b = node(half * HALF + jj, VY)
        return a, b

    def first_chunk(c, group, half):
        bstep = 1 if half else -1

        def body(jj, carry):
            a, b = node_ab(group, half, jj)
            abs_a, abs_b = jnp.abs(a), jnp.abs(b)
            parts = poly_parts(fields, a, b)
            amask = abs_a * off_edge
            base = (c * HALF + jj) * (VZ * ROWS)
            for k in range(VZ // 2, VZ):
                cv = node_c(k)
                src = poly_pair(parts, cv)
                w = pore / (jnp.full((ROWS, LANES), 1.0 + abs_a + abs_b, jnp.float32) + cv)
                for sign in range(2):
                    kk = k if sign else VZ - 1 - k
                    rows = pl.ds(pl.multiple_of(base, ROWS) + kk * ROWS, ROWS)
                    f = f_ref[rows, :]
                    h_ref[rows, :] = sweep(
                        f, src[sign], w, amask, abs_b, cv, bstep, 1 if sign else -1
                    )
            return carry

        lax.fori_loop(0, HALF, body, 0)

    def second_chunk(c, group, half):
        bstep = 1 if half else -1

        def body(jj, carry):
            a, b = node_ab(group, half, jj)
            abs_a, abs_b = jnp.abs(a), jnp.abs(b)
            parts = poly_parts(fields, a, b)
            amask = abs_a * off_edge
            aedge = abs_a * at_edge
            base = (c * HALF + jj) * (VZ * ROWS)
            hbase = (c * HALF + jj) * (VZ * 2)
            s0 = s1 = s2 = s3 = None
            for k in range(VZ // 2, VZ):
                cv = node_c(k)
                src = poly_pair(parts, cv)
                w = pore / (jnp.full((ROWS, LANES), 1.0 + abs_a + abs_b, jnp.float32) + cv)
                wa = w * aedge
                got = []
                for sign in range(2):
                    kk = k if sign else VZ - 1 - k
                    rows = pl.ds(pl.multiple_of(base, ROWS) + kk * ROWS, ROWS)

                    def halo(ref):
                        at = pl.multiple_of(hbase, ROWS) + kk * 2
                        lower = jnp.broadcast_to(ref[pl.ds(at, 1), :], (ROWS, LANES))
                        upper = jnp.broadcast_to(ref[pl.ds(at + 1, 1), :], (ROWS, LANES))
                        return jnp.where(row < ROWS // 2, lower, upper)

                    h = h_ref[rows, :] + wa * halo(frecv)
                    total = sweep(h, src[sign], w, amask, abs_b, cv, bstep, 1 if sign else -1)
                    total = total + wa * halo(hrecv)
                    g_ref[rows, :] = total
                    got.append(total)
                u = got[1] + got[0]
                d = got[1] - got[0]
                if s0 is None:
                    s0, s1, s2, s3 = u, cv * d, (cv * cv) * u, (cv**3) * d
                else:
                    s0, s1 = s0 + u, s1 + cv * d
                    s2, s3 = s2 + (cv * cv) * u, s3 + (cv**3) * d
            q = a * a + b * b
            heat = (q - 2.5) * s0 + s2
            terms = (
                s0, a * s0, b * s0, s1, (q - 1.5) * s0 + s2,
                a * heat, b * heat, (q - 2.5) * s1 + s3, (a * b) * s0, b * s1,
            )
            for m, term in enumerate(terms):
                rows = pl.ds(m * ROWS, ROWS)
                acc[rows, :] = acc[rows, :] + term
            return carry

        lax.fori_loop(0, HALF, body, 0)

    def store(c):
        rows = pl.ds(c * (CHUNK * ROWS), CHUNK * ROWS)
        return pltpu.make_async_copy(g_ref.at[rows], half_hbm.at[rows], out_sem.at[c])

    pl.semaphore_wait(barrier, nvel + 1)
    pores = edges(pore_ext, pore_ext, ps_sem, pr_sem)
    for copy in pores:
        copy.start()

    def phase_one(group, carry):
        for half in range(2):
            c = group * 2 + half
            load(c).wait()
            pack_chunk(f_ref, fsend, c)
            send(fsend, frecv, fs_sem, fr_sem, c).start()
            first_chunk(c, group, half)
            pack_chunk(h_ref, hsend, c)
            send(hsend, hrecv, hs_sem, hr_sem, c).start()
        return carry

    lax.fori_loop(0, groups, phase_one, 0)

    def phase_two(group, carry):
        for half in range(2):
            c = group * 2 + half
            send(fsend, frecv, fs_sem, fr_sem, c).wait_recv()
            send(hsend, hrecv, hs_sem, hr_sem, c).wait_recv()
            second_chunk(c, group, half)
            store(c).start()
        return carry

    lax.fori_loop(0, groups, phase_two, 0)

    mrecv[vel] = acc[...] * volume

    def moment_copy(d, slot):
        return pltpu.make_async_remote_copy(
            src_ref=mrecv.at[vel], dst_ref=mrecv.at[slot],
            send_sem=ms_sem.at[d - 1], recv_sem=mr_sem.at[slot],
            device_id={"vel": lax.rem(vel + d, nvel)}, device_id_type=MESH,
        )

    for d in range(1, nvel):
        moment_copy(d, vel).start()
    for d in range(1, nvel):
        moment_copy(d, lax.rem(vel + d, nvel)).wait_recv()
    total = mrecv[0]
    for s in range(1, nvel):
        total = total + mrecv[s]
    mnew_ref[...] = total
    change_ext[1] = total - m_ref[...]
    changes = edges(change_ext, change_ext, cs_sem, cr_sem)
    for copy in changes:
        copy.start()
    for copy in pores:
        copy.wait()
    for copy in changes:
        copy.wait_recv()

    first = plane == 0
    final = plane == ROWS // 2 - 1
    up = ROWS - ROWS // 2 + 1
    down = ROWS // 2 - 1
    porous = [pore_ext[s] for s in range(3)]

    def relax(m, carry):
        rows = pl.ds(pl.multiple_of(m * ROWS, ROWS), ROWS)
        scale = 1.0 / jnp.full((ROWS, LANES), rate_ref[m] + 6.0, jnp.float32)
        forcing = [change_ext[s, rows, :] for s in range(3)]
        gain = [porous[s] * scale for s in range(3)]
        value = [gain[s] * forcing[s] for s in range(3)]
        for step in range(SWEEPS - 1):
            fresh = list(value)
            for s in (range(3) if step < SWEEPS - 2 else (1,)):
                v = value[s]
                before = pltpu.roll(v, 1, 0)
                after = pltpu.roll(v, ROWS - 1, 0)
                if s > 0:
                    before = jnp.where(first, pltpu.roll(value[s - 1], up, 0), before)
                if s < 2:
                    after = jnp.where(final, pltpu.roll(value[s + 1], down, 0), after)
                beside = from_y(v, 1, lane) + from_y(v, -1, lane)
                beside = beside + from_z(v, 1, lane) + from_z(v, -1, lane)
                fresh[s] = gain[s] * (forcing[s] + (before + after + beside))
            value = fresh
        mnew_ref[rows, :] = mnew_ref[rows, :] + value[1]
        corr_ref[rows, :] = value[1]
        return carry

    lax.fori_loop(0, NMOM, relax, 0)

    for copy in changes:
        copy.wait_send()
    for d in range(1, nvel):
        moment_copy(d, vel).wait_send()

    def finish(c, carry):
        send(fsend, frecv, fs_sem, fr_sem, c).wait_send()
        send(hsend, hrecv, hs_sem, hr_sem, c).wait_send()
        store(c).wait()
        return carry

    lax.fori_loop(0, chunks, finish, 0)


def lift_kernel(groups, half_ref, corr_ref, pore_ref, out_ref):
    step = pl.program_id(0)
    vel = lax.axis_index("vel")
    pore = pore_ref[...].astype(jnp.float32)
    fields = [pore * corr_ref[pl.ds(m * ROWS, ROWS), :] for m in range(NMOM)]

    def body(jj, carry):
        a = node(vel * groups + step // 2, VX)
        b = node(lax.rem(step, 2) * HALF + jj, VY)
        parts = poly_parts(fields, a, b)
        base = pl.multiple_of(jj * (VZ * ROWS), ROWS)
        for k in range(VZ // 2, VZ):
            lifted = poly_pair(parts, node_c(k))
            for sign in range(2):
                kk = k if sign else VZ - 1 - k
                rows = pl.ds(base + kk * ROWS, ROWS)
                out_ref[rows, :] = half_ref[rows, :] + lifted[sign]
        return carry

    lax.fori_loop(0, HALF, body, 0)


def to_rows(x):
    lead, thickness, cells = x.shape
    parts = cells // LANES
    return x.reshape(lead, thickness, parts, LANES).transpose(0, 2, 1, 3).reshape(-1, LANES)


def from_rows(x, lead, thickness, cells):
    parts = cells // LANES
    return x.reshape(lead, parts, thickness, LANES).transpose(0, 2, 1, 3).reshape(lead, thickness, cells)


def body(nvel, nspace, distribution, moments_old, pore_mask, synthetic_rate):
    velocities, thickness, cells = distribution.shape
    groups = velocities // (VY * VZ)
    assert thickness * cells == ROWS * LANES and nvel % 2 == 0 and thickness >= SWEEPS - 1
    rows = to_rows(distribution)
    old = to_rows(moments_old)
    pore = to_rows(pore_mask[None])
    chunks = groups * 2
    total = velocities * ROWS
    vmem = pl.BlockSpec(memory_space=pltpu.VMEM)
    anyspace = pl.BlockSpec(memory_space=pl.ANY)
    f32 = jnp.float32
    dma = pltpu.SemaphoreType.DMA
    half, moments_new, correction = pl.pallas_call(
        functools.partial(transport_kernel, nvel, nspace, groups),
        out_shape=(
            jax.ShapeDtypeStruct((total, LANES), f32),
            jax.ShapeDtypeStruct((NMOM * ROWS, LANES), f32),
            jax.ShapeDtypeStruct((NMOM * ROWS, LANES), f32),
        ),
        in_specs=[anyspace, vmem, vmem, pl.BlockSpec(memory_space=pltpu.SMEM)],
        out_specs=(anyspace, vmem, vmem),
        scratch_shapes=[
            pltpu.VMEM((total, LANES), f32),
            pltpu.VMEM((total, LANES), f32),
            pltpu.VMEM((total, LANES), f32),
            pltpu.VMEM((velocities * 2, LANES), f32),
            pltpu.VMEM((velocities * 2, LANES), f32),
            pltpu.VMEM((velocities * 2, LANES), f32),
            pltpu.VMEM((velocities * 2, LANES), f32),
            pltpu.VMEM((NMOM * ROWS, LANES), f32),
            pltpu.VMEM((nvel, NMOM * ROWS, LANES), f32),
            pltpu.VMEM((3, ROWS, LANES), f32),
            pltpu.VMEM((3, NMOM * ROWS, LANES), f32),
            dma((chunks,)), dma((chunks,)), dma((chunks,)), dma((chunks,)), dma((chunks,)), dma((chunks,)),
            dma((nvel - 1,)), dma((nvel,)), dma((2,)), dma((2,)), dma((2,)), dma((2,)),
        ],
        compiler_params=pltpu.CompilerParams(
            collective_id=0, has_side_effects=True, vmem_limit_bytes=24 * 1024 * 1024
        ),
        name="transport",
    )(rows, old, pore, synthetic_rate)
    fixed = lambda c: (0, 0)
    moving = pl.BlockSpec((CHUNK * ROWS, LANES), lambda c: (c, 0))
    new = pl.pallas_call(
        functools.partial(lift_kernel, groups),
        out_shape=jax.ShapeDtypeStruct((total, LANES), f32),
        grid=(chunks,),
        in_specs=[
            moving,
            pl.BlockSpec((NMOM * ROWS, LANES), fixed),
            pl.BlockSpec((ROWS, LANES), fixed),
        ],
        out_specs=moving,
        name="lift",
    )(half, correction, pore)
    return (
        from_rows(new, velocities, thickness, cells),
        from_rows(moments_new, NMOM, thickness, cells),
    )


def solution(mesh):
    placed = (P("vel", "space", None), P(None, "space", None), P("space", None), P())
    return jax.shard_map(
        functools.partial(body, mesh.shape["vel"], mesh.shape["space"]),
        mesh=mesh,
        in_specs=placed,
        out_specs=(P("vel", "space", None), P(None, "space", None)),
        check_vma=False,
    )
```

time: 140 us -> 46.2 us (0.33)
  local copies, waits for them, and re-layouts: 51.4 us -> 6.41 us
  Pallas kernels: 0 us -> 38.7 us
  other arithmetic: 27.6 us -> 0 us
  starting transfers between devices: 22.5 us -> 0 us
  blocking collectives: 17.9 us -> 0 us
  matrix products: 13.8 us -> 0 us
  waiting for transfers between devices: 5.17 us -> 0 us
    pallas_call x0 -> x2, Pallas kernels: none -> 38.7 us  [the longest x1 32.4 us: body(): pl.pallas_call(functools.partial(transport_kernel, nvel, nspace, groups),...]
    concatenate x8 -> x0, local copies, waits for them, and re-layouts: 23.1 us -> none  [the longest x2 6.39 us: upwind_sweep(): jnp.roll(cube_view, 1, 2)]
    ppermute x12 -> x0, starting transfers between devices: 22.5 us -> none  [the longest x6 21.8 us: padded_2(): lax.ppermute(head, axis, [((i + 1) % count, i) for i in range(count)])]
    concatenate x6 -> x0, other arithmetic: 19.6 us -> none  [the longest x2 7.8 us: upwind_sweep(): jnp.roll(cube_view, 1, 2)]
    psum x1 -> x0, blocking collectives: 17.9 us -> none  [body(): moments_half = lax.psum(partial_value, 'vel')]
    slice x30 -> x0, local copies, waits for them, and re-layouts: 14.3 us -> none  [the longest x4 5.79 us: upwind_sweep(): jnp.roll(cube_view, -1, 3)]
    dot_general x3 -> x0, matrix products: 13.8 us -> none  [the longest x2 12.6 us: lift(): jnp.dot(spread_rows, fields.reshape(moment_count, -1), precision=lax.Prec...]
    div x5 -> x0, other arithmetic: 6.62 us -> none  [the longest x1 6.31 us: upwind_sweep(): porous[None] * (collide * source + inflow) / denominator[:, None, None]]
  transfers between devices with their start and end apart: 12 -> 0, of which waited for: 8 -> 0; matrix products, arithmetic and copies ran while one was open for 31% -> 0% of each run, Pallas kernels for 0% -> 0%
where the time goes in v1:
time: 46.2 us; the launch traced here: 45.8 us
  Pallas kernels  38.7 us (84%)
  local copies, waits for them, and re-layouts  6.41 us (14%)
  between operations  0.66 us (1%)
    pallas_call x1, Pallas kernels, body(): pl.pallas_call(functools.partial(transport_kernel, nvel, nspace, groups),...  32.4 us
    unnamed x13, local copies, waits for them, and re-layouts  6.41 us
    pallas_call x1, Pallas kernels, body(): pl.pallas_call(functools.partial(lift_kernel, groups), out_shape=jax.Shap...  6.34 us

profile of v1, /device:TPU:0, one launch (start us, length us, event | category | flops | bytes accessed | tf_op | source)
XLA Modules:
  0.0 45.8 jit_solution(4080338988920952000)
XLA Ops:
  0.6 0.0 copy-start
  0.6 1.7 %copy-done = f32[576,4,256]{2,1,0:T(4,128)S(1)} copy-done((f32[576,4,256]{2,1,0:T(4,128)S(1)}, f32[576,4,256]{2,1,0:T(4,128)}, u32[]{:S(2)}) %copy-start) | copy-done | bytes 2359320
  2.3 0.0 copy-start.3
  2.3 0.8 %copy-done.3 = f32[10,4,256]{2,1,0:T(4,128)S(1)} copy-done((f32[10,4,256]{2,1,0:T(4,128)S(1)}, f32[10,4,256]{2,1,0:T(4,128)}, u32[]{:S(2)}) %copy-start.3) | copy-done | bytes 40984
  3.1 0.0 copy-start.4
  3.1 0.7 %copy-done.4 = s32[4,256]{1,0:T(4,128)S(1)} copy-done((s32[4,256]{1,0:T(4,128)S(1)}, s32[4,256]{1,0:T(4,128)}, u32[]{:S(2)}) %copy-start.4) | copy-done | bytes 4120
  3.8 0.0 copy-start.5
  3.8 0.7 %copy-done.5 = f32[10]{0:T(128)S(1)} copy-done((f32[10]{0:T(128)S(1)}, f32[10]{0:T(128)}, u32[]{:S(2)}) %copy-start.5) | copy-done | bytes 64
  4.4 32.4 %transport.1 = (f32[4608,128]{1,0:T(8,128)S(1)}, f32[80,128]{1,0:T(8,128)S(1)}, f32[80,128]{1,0:T(8,128)S(1)}) custom-call(f32[4608,128]{1,0:T(8,128)S(1)} %bitcast.25, f32[80,128]{1,0:T(8,128)S(1)} %bitcast.27, s32[8,128]{1,0:T(8,128)S(1)} %bitcast.29, f32[10]{0:T(128)S(1)} %copy-done.5), custom_call_target="tpu_custom_call" | custom-call | tf_op jit(solution)/shard_map/transport/pallas_call | solution.py:397
  36.8 0.0 copy-start.1
  36.8 1.4 %copy-done.1 = f32[4608,128]{1,0:T(8,128)} copy-done((f32[4608,128]{1,0:T(8,128)}, f32[4608,128]{1,0:T(8,128)S(1)}, u32[]{:S(2)}) %copy-start.1) | copy-done | bytes 2359320
  38.2 0.0 copy-start.2
  38.2 0.6 %copy-done.2 = f32[80,128]{1,0:T(8,128)} copy-done((f32[80,128]{1,0:T(8,128)}, f32[80,128]{1,0:T(8,128)S(1)}, u32[]{:S(2)}) %copy-start.2) | copy-done | bytes 40984
  38.9 6.3 %lift.1 = f32[4608,128]{1,0:T(8,128)} custom-call(f32[4608,128]{1,0:T(8,128)} %copy-done.1, f32[80,128]{1,0:T(8,128)} %copy-done.2, s32[8,128]{1,0:T(8,128)} %bitcast.28), custom_call_target="tpu_custom_call" | custom-call | tf_op jit(solution)/shard_map/lift/pallas_call | solution.py:428
  45.2 0.6 %copy.12 = f32[10,4,256]{2,1,0:T(4,128)} copy(f32[10,4,256]{2,1,0:T(4,128)S(1)} %bitcast.26) | data formatting | bytes 81920
Async XLA Ops:
  0.6 1.7 %copy-start = (f32[576,4,256]{2,1,0:T(4,128)S(1)}, f32[576,4,256]{2,1,0:T(4,128)}, u32[]{:S(2)}) copy-start(f32[576,4,256]{2,1,0:T(4,128)} %param.4) | copy-start | bytes 7077892
  2.3 0.8 %copy-start.3 = (f32[10,4,256]{2,1,0:T(4,128)S(1)}, f32[10,4,256]{2,1,0:T(4,128)}, u32[]{:S(2)}) copy-start(f32[10,4,256]{2,1,0:T(4,128)} %param.5) | copy-start | bytes 122884
  3.1 0.7 %copy-start.4 = (s32[4,256]{1,0:T(4,128)S(1)}, s32[4,256]{1,0:T(4,128)}, u32[]{:S(2)}) copy-start(s32[4,256]{1,0:T(4,128)} %param.6) | copy-start | bytes 12292
  3.8 0.7 %copy-start.5 = (f32[10]{0:T(128)S(1)}, f32[10]{0:T(128)}, u32[]{:S(2)}) copy-start(f32[10]{0:T(128)} %rate_ref.1) | copy-start | bytes 124
  36.8 1.4 %copy-start.1 = (f32[4608,128]{1,0:T(8,128)}, f32[4608,128]{1,0:T(8,128)S(1)}, u32[]{:S(2)}) copy-start(f32[4608,128]{1,0:T(8,128)S(1)} %get-tuple-element.5.half_ref) | copy-start | bytes 7077892
  38.2 0.6 %copy-start.2 = (f32[80,128]{1,0:T(8,128)}, f32[80,128]{1,0:T(8,128)S(1)}, u32[]{:S(2)}) copy-start(f32[80,128]{1,0:T(8,128)S(1)} %get-tuple-element.6.corr_ref) | copy-start | bytes 122884

commit v2 on v1

--- a/solution.py
+++ b/solution.py
@@ -84,11 +84,11 @@
 
 def transport_kernel(
     nvel, nspace, groups,
-    f_hbm, m_ref, pore_ref, rate_ref,
-    half_hbm, mnew_ref, corr_ref,
-    f_ref, h_ref, g_ref, fsend, hsend, frecv, hrecv,
+    f_hbm, m_hbm, pore_hbm, rate_hbm,
+    g_ref, mnew_ref, corr_ref,
+    f_ref, h_ref, m_ref, pore_ref, rate_ref, fsend, hsend, frecv, hrecv,
     acc, mrecv, pore_ext, change_ext,
-    in_sem, out_sem, fs_sem, fr_sem, hs_sem, hr_sem, ms_sem, mr_sem, ps_sem, pr_sem, cs_sem, cr_sem,
+    in_sem, small_sem, fs_sem, fr_sem, hs_sem, hr_sem, ms_sem, mr_sem, ps_sem, pr_sem, cs_sem, cr_sem,
 ):
     vel = lax.axis_index("vel")
     space = lax.axis_index("space")
@@ -103,8 +103,16 @@
         rows = pl.ds(c * (CHUNK * ROWS), CHUNK * ROWS)
         return pltpu.make_async_copy(f_hbm.at[rows], f_ref.at[rows], in_sem.at[c])
 
+    small = [
+        pltpu.make_async_copy(src, dst, small_sem.at[n])
+        for n, (src, dst) in enumerate(
+            ((m_hbm, m_ref), (pore_hbm, pore_ref), (rate_hbm, rate_ref))
+        )
+    ]
     for c in range(chunks):
         load(c).start()
+    for copy in small:
+        copy.start()
 
     barrier = pltpu.get_barrier_semaphore()
     for other in (left, right):
@@ -116,6 +124,8 @@
 
     lane, row = masks()
     plane = lax.rem(row, ROWS // 2)
+    for copy in small:
+        copy.wait()
     pore = pore_ref[...].astype(jnp.float32)
     pore_ext[1] = pore
     edge = jnp.where(positive, 0, ROWS // 2 - 1)
@@ -243,11 +253,20 @@
 
         lax.fori_loop(0, HALF, body, 0)
 
-    def store(c):
-        rows = pl.ds(c * (CHUNK * ROWS), CHUNK * ROWS)
-        return pltpu.make_async_copy(g_ref.at[rows], half_hbm.at[rows], out_sem.at[c])
+    def prepare(c, carry):
+        load(c).wait()
+        pack_chunk(f_ref, fsend, c)
+        return carry
+
+    lax.fori_loop(0, chunks, prepare, 0)
 
     pl.semaphore_wait(barrier, nvel + 1)
+
+    def send_first(c, carry):
+        send(fsend, frecv, fs_sem, fr_sem, c).start()
+        return carry
+
+    lax.fori_loop(0, chunks, send_first, 0)
     pores = edges(pore_ext, pore_ext, ps_sem, pr_sem)
     for copy in pores:
         copy.start()
@@ -255,9 +274,6 @@
     def phase_one(group, carry):
         for half in range(2):
             c = group * 2 + half
-            load(c).wait()
-            pack_chunk(f_ref, fsend, c)
-            send(fsend, frecv, fs_sem, fr_sem, c).start()
             first_chunk(c, group, half)
             pack_chunk(h_ref, hsend, c)
             send(hsend, hrecv, hs_sem, hr_sem, c).start()
@@ -271,7 +287,6 @@
             send(fsend, frecv, fs_sem, fr_sem, c).wait_recv()
             send(hsend, hrecv, hs_sem, hr_sem, c).wait_recv()
             second_chunk(c, group, half)
-            store(c).start()
         return carry
 
     lax.fori_loop(0, groups, phase_two, 0)
@@ -308,8 +323,8 @@
     down = ROWS // 2 - 1
     porous = [pore_ext[s] for s in range(3)]
 
-    def relax(m, carry):
-        rows = pl.ds(pl.multiple_of(m * ROWS, ROWS), ROWS)
+    for m in range(NMOM):
+        rows = pl.ds(m * ROWS, ROWS)
         scale = 1.0 / jnp.full((ROWS, LANES), rate_ref[m] + 6.0, jnp.float32)
         forcing = [change_ext[s, rows, :] for s in range(3)]
         gain = [porous[s] * scale for s in range(3)]
@@ -329,10 +344,7 @@
                 fresh[s] = gain[s] * (forcing[s] + (before + after + beside))
             value = fresh
         mnew_ref[rows, :] = mnew_ref[rows, :] + value[1]
-        corr_ref[rows, :] = value[1]
-        return carry
-
-    lax.fori_loop(0, NMOM, relax, 0)
+        corr_ref[rows, :] = pore * value[1]
 
     for copy in changes:
         copy.wait_send()
@@ -342,32 +354,75 @@
     def finish(c, carry):
         send(fsend, frecv, fs_sem, fr_sem, c).wait_send()
         send(hsend, hrecv, hs_sem, hr_sem, c).wait_send()
-        store(c).wait()
         return carry
 
     lax.fori_loop(0, chunks, finish, 0)
 
 
-def lift_kernel(groups, half_ref, corr_ref, pore_ref, out_ref):
-    step = pl.program_id(0)
+def group_parts(m, a):
+    k = coefficients
+    a = jnp.full((ROWS, LANES), a, jnp.float32)
+    a2 = a * a
+    weight = jnp.exp(-a2)
+    bb = k[4] * m[4] + (k[5] * a) * m[5]
+    one = k[0] * m[0] + (k[1] * a) * m[1] + (k[4] * (a2 - 1.5)) * m[4] + (k[5] * a * (a2 - 2.5)) * m[5]
+    b1 = k[2] * m[2] + (k[6] * (a2 - 2.5)) * m[6] + (k[8] * a) * m[8]
+    c1 = k[3] * m[3] + (k[7] * (a2 - 2.5)) * m[7]
+    return [weight * x for x in (one, b1, bb, k[6] * m[6], c1, k[9] * m[9], k[7] * m[7])]
+
+
+def pair_parts(parts, b):
+    one, b1, bb, bbb, c1, cb, cbb = parts
+    g = math.exp(-b * b)
+    p0e, p0o = g * one + (g * b * b) * bb, (g * b) * b1 + (g * b**3) * bbb
+    p1e, p1o = g * c1 + (g * b * b) * cbb, (g * b) * cb
+    p2e, p2o = g * bb, (g * b) * bbb
+    p3 = g * cbb
+    return (
+        (p0e - p0o, p1e - p1o, p2e - p2o, p3),
+        (p0e + p0o, p1e + p1o, p2e + p2o, p3),
+    )
+
+
+def node_b(j):
+    return -extent + (j + 0.5) * (2.0 * extent / VY)
+
+
+def lift_kernel(groups, half_ref, corr_ref, mnew_ref, out_hbm, mout_hbm, stage, sem, msem):
     vel = lax.axis_index("vel")
-    pore = pore_ref[...].astype(jnp.float32)
-    fields = [pore * corr_ref[pl.ds(m * ROWS, ROWS), :] for m in range(NMOM)]
-
-    def body(jj, carry):
-        a = node(vel * groups + step // 2, VX)
-        b = node(lax.rem(step, 2) * HALF + jj, VY)
-        parts = poly_parts(fields, a, b)
-        base = pl.multiple_of(jj * (VZ * ROWS), ROWS)
-        for k in range(VZ // 2, VZ):
-            lifted = poly_pair(parts, node_c(k))
-            for sign in range(2):
-                kk = k if sign else VZ - 1 - k
-                rows = pl.ds(base + kk * ROWS, ROWS)
-                out_ref[rows, :] = half_ref[rows, :] + lifted[sign]
-        return carry
-
-    lax.fori_loop(0, HALF, body, 0)
+    size = VY * VZ * ROWS
+    moments = pltpu.make_async_copy(mnew_ref, mout_hbm, msem)
+    moments.start()
+
+    def store(g):
+        rows = pl.ds(g * size, size)
+        return pltpu.make_async_copy(stage.at[rows], out_hbm.at[rows], sem.at[g])
+
+    def body(g, carry):
+        fields = [corr_ref[pl.ds(m * ROWS, ROWS), :] for m in range(NMOM)]
+        parts = group_parts(fields, node(vel * groups + g, VX))
+        base = pl.multiple_of(g * size, ROWS)
+        for j in range(HALF, VY):
+            both = pair_parts(parts, node_b(j))
+            for bsign in range(2):
+                jj = j if bsign else VY - 1 - j
+                for k in range(VZ // 2, VZ):
+                    lifted = poly_pair(both[bsign], node_c(k))
+                    for sign in range(2):
+                        kk = k if sign else VZ - 1 - k
+                        rows = pl.ds(base + (jj * VZ + kk) * ROWS, ROWS)
+                        stage[rows, :] = half_ref[rows, :] + lifted[sign]
+        store(g).start()
+        return carry
+
+    lax.fori_loop(0, groups, body, 0)
+
+    def finish(g, carry):
+        store(g).wait()
+        return carry
+
+    lax.fori_loop(0, groups, finish, 0)
+    moments.wait()
 
 
 def to_rows(x):
@@ -391,7 +446,7 @@
     chunks = groups * 2
     total = velocities * ROWS
     vmem = pl.BlockSpec(memory_space=pltpu.VMEM)
-    anyspace = pl.BlockSpec(memory_space=pl.ANY)
+    hbm = pl.BlockSpec(memory_space=pltpu.HBM)
     f32 = jnp.float32
     dma = pltpu.SemaphoreType.DMA
     half, moments_new, correction = pl.pallas_call(
@@ -401,12 +456,14 @@
             jax.ShapeDtypeStruct((NMOM * ROWS, LANES), f32),
             jax.ShapeDtypeStruct((NMOM * ROWS, LANES), f32),
         ),
-        in_specs=[anyspace, vmem, vmem, pl.BlockSpec(memory_space=pltpu.SMEM)],
-        out_specs=(anyspace, vmem, vmem),
+        in_specs=[hbm] * 4,
+        out_specs=(vmem,) * 3,
         scratch_shapes=[
             pltpu.VMEM((total, LANES), f32),
             pltpu.VMEM((total, LANES), f32),
-            pltpu.VMEM((total, LANES), f32),
+            pltpu.VMEM((NMOM * ROWS, LANES), f32),
+            pltpu.VMEM((ROWS, LANES), jnp.int32),
+            pltpu.SMEM((NMOM,), f32),
             pltpu.VMEM((velocities * 2, LANES), f32),
             pltpu.VMEM((velocities * 2, LANES), f32),
             pltpu.VMEM((velocities * 2, LANES), f32),
@@ -415,7 +472,7 @@
             pltpu.VMEM((nvel, NMOM * ROWS, LANES), f32),
             pltpu.VMEM((3, ROWS, LANES), f32),
             pltpu.VMEM((3, NMOM * ROWS, LANES), f32),
-            dma((chunks,)), dma((chunks,)), dma((chunks,)), dma((chunks,)), dma((chunks,)), dma((chunks,)),
+            dma((chunks,)), dma((3,)), dma((chunks,)), dma((chunks,)), dma((chunks,)), dma((chunks,)),
             dma((nvel - 1,)), dma((nvel,)), dma((2,)), dma((2,)), dma((2,)), dma((2,)),
         ],
         compiler_params=pltpu.CompilerParams(
@@ -423,23 +480,21 @@
         ),
         name="transport",
     )(rows, old, pore, synthetic_rate)
-    fixed = lambda c: (0, 0)
-    moving = pl.BlockSpec((CHUNK * ROWS, LANES), lambda c: (c, 0))
-    new = pl.pallas_call(
+    new, moments_out = pl.pallas_call(
         functools.partial(lift_kernel, groups),
-        out_shape=jax.ShapeDtypeStruct((total, LANES), f32),
-        grid=(chunks,),
-        in_specs=[
-            moving,
-            pl.BlockSpec((NMOM * ROWS, LANES), fixed),
-            pl.BlockSpec((ROWS, LANES), fixed),
-        ],
-        out_specs=moving,
+        out_shape=(
+            jax.ShapeDtypeStruct((total, LANES), f32),
+            jax.ShapeDtypeStruct((NMOM * ROWS, LANES), f32),
+        ),
+        in_specs=[vmem] * 3,
+        out_specs=(hbm,) * 2,
+        scratch_shapes=[pltpu.VMEM((total, LANES), f32), dma((groups,)), dma(())],
+        compiler_params=pltpu.CompilerParams(vmem_limit_bytes=12 * 1024 * 1024),
         name="lift",
-    )(half, correction, pore)
+    )(half, correction, moments_new)
     return (
         from_rows(new, velocities, thickness, cells),
-        from_rows(moments_new, NMOM, thickness, cells),
+        from_rows(moments_out, NMOM, thickness, cells),
     )
 
 

time: 46.2 us -> 36.7 us (0.79)
  Pallas kernels: 38.7 us -> 32 us
  local copies, waits for them, and re-layouts: 6.41 us -> 3.78 us
    pallas_call x1, Pallas kernels: 6.34 us -> 1.58 us  [body(): pl.pallas_call(functools.partial(lift_kernel, groups), out_shape=(jax.Sha...]
    unnamed x13 -> x8, local copies, waits for them, and re-layouts: 6.41 us -> 3.78 us
    pallas_call x1, Pallas kernels: 32.4 us -> 30.4 us  [body(): pl.pallas_call(functools.partial(transport_kernel, nvel, nspace, groups),...]
where the time goes in v2:
time: 36.7 us; the launch traced here: 36.5 us
  Pallas kernels  32 us (87%)
  local copies, waits for them, and re-layouts  3.78 us (10%)
  between operations  0.65 us (2%)
    pallas_call x1, Pallas kernels, body(): pl.pallas_call(functools.partial(transport_kernel, nvel, nspace, groups),...  30.4 us
    unnamed x8, local copies, waits for them, and re-layouts  3.78 us
    pallas_call x1, Pallas kernels, body(): pl.pallas_call(functools.partial(lift_kernel, groups), out_shape=(jax.Sha...  1.58 us

profile of v2, /device:TPU:0, one launch (start us, length us, event | category | flops | bytes accessed | tf_op | source)
XLA Modules:
  0.0 36.5 jit_solution(10649398906650606011)
XLA Ops:
  0.6 0.0 copy-start
  0.6 1.7 %copy-done = f32[576,4,256]{2,1,0:T(4,128)S(1)} copy-done((f32[576,4,256]{2,1,0:T(4,128)S(1)}, f32[576,4,256]{2,1,0:T(4,128)}, u32[]{:S(2)}) %copy-start) | copy-done | bytes 2359320
  2.3 0.0 copy-start.1
  2.3 0.8 %copy-done.1 = f32[10,4,256]{2,1,0:T(4,128)S(1)} copy-done((f32[10,4,256]{2,1,0:T(4,128)S(1)}, f32[10,4,256]{2,1,0:T(4,128)}, u32[]{:S(2)}) %copy-start.1) | copy-done | bytes 40984
  3.1 0.0 copy-start.2
  3.1 0.7 %copy-done.2 = s32[4,256]{1,0:T(4,128)S(1)} copy-done((s32[4,256]{1,0:T(4,128)S(1)}, s32[4,256]{1,0:T(4,128)}, u32[]{:S(2)}) %copy-start.2) | copy-done | bytes 4120
  3.8 0.0 copy-start.3
  3.8 0.7 %copy-done.3 = f32[10]{0:T(128)S(1)} copy-done((f32[10]{0:T(128)S(1)}, f32[10]{0:T(128)}, u32[]{:S(2)}) %copy-start.3) | copy-done | bytes 64
  4.4 30.4 %transport.1 = (f32[4608,128]{1,0:T(8,128)S(1)}, f32[80,128]{1,0:T(8,128)S(1)}, f32[80,128]{1,0:T(8,128)S(1)}) custom-call(f32[4608,128]{1,0:T(8,128)S(1)} %bitcast.25, f32[80,128]{1,0:T(8,128)S(1)} %bitcast.26, s32[8,128]{1,0:T(8,128)S(1)} %bitcast.27, f32[10]{0:T(128)S(1)} %copy-done.3), custom_call_target="tpu_custom_call" | custom-call | tf_op jit(solution)/shard_map/transport/pallas_call | solution.py:452
  34.9 1.6 %lift.1 = (f32[4608,128]{1,0:T(8,128)}, f32[80,128]{1,0:T(8,128)}) custom-call(f32[4608,128]{1,0:T(8,128)S(1)} %get-tuple-element.7.half_ref, f32[80,128]{1,0:T(8,128)S(1)} %get-tuple-element.8.corr_ref, f32[80,128]{1,0:T(8,128)S(1)} %get-tuple-element.9.mnew_ref), custom_call_target="tpu_custom_call" | custom-call | tf_op jit(solution)/shard_map/lift/pallas_call | solution.py:483
Async XLA Ops:
  0.6 1.7 %copy-start = (f32[576,4,256]{2,1,0:T(4,128)S(1)}, f32[576,4,256]{2,1,0:T(4,128)}, u32[]{:S(2)}) copy-start(f32[576,4,256]{2,1,0:T(4,128)} %param.4) | copy-start | bytes 7077892
  2.3 0.8 %copy-start.1 = (f32[10,4,256]{2,1,0:T(4,128)S(1)}, f32[10,4,256]{2,1,0:T(4,128)}, u32[]{:S(2)}) copy-start(f32[10,4,256]{2,1,0:T(4,128)} %param.5) | copy-start | bytes 122884
  3.1 0.7 %copy-start.2 = (s32[4,256]{1,0:T(4,128)S(1)}, s32[4,256]{1,0:T(4,128)}, u32[]{:S(2)}) copy-start(s32[4,256]{1,0:T(4,128)} %param.6) | copy-start | bytes 12292
  3.8 0.7 %copy-start.3 = (f32[10]{0:T(128)S(1)}, f32[10]{0:T(128)}, u32[]{:S(2)}) copy-start(f32[10]{0:T(128)} %rate_hbm.1) | copy-start | bytes 124

commit v3 on v2

--- a/solution.py
+++ b/solution.py
@@ -479,7 +479,7 @@
             collective_id=0, has_side_effects=True, vmem_limit_bytes=24 * 1024 * 1024
         ),
         name="transport",
-    )(rows, old, pore, synthetic_rate)
+    )(*(pltpu.with_memory_space_constraint(x, pltpu.HBM) for x in (rows, old, pore, synthetic_rate)))
     new, moments_out = pl.pallas_call(
         functools.partial(lift_kernel, groups),
         out_shape=(

time: 36.7 us -> 32.3 us (0.88)
  local copies, waits for them, and re-layouts: 3.78 us -> 0 us
  Pallas kernels: 32 us -> 31.5 us
    unnamed x8 -> x0, local copies, waits for them, and re-layouts: 3.78 us -> none
    pallas_call x1, Pallas kernels: 30.4 us -> 30 us  [body(): pl.pallas_call(functools.partial(transport_kernel, nvel, nspace, groups),...]
where the time goes in v3:
time: 32.3 us; the launch traced here: 32.2 us
  Pallas kernels  31.5 us (98%)
  between operations  0.64 us (2%)
    pallas_call x1, Pallas kernels, body(): pl.pallas_call(functools.partial(transport_kernel, nvel, nspace, groups),...  30 us
    pallas_call x1, Pallas kernels, body(): pl.pallas_call(functools.partial(lift_kernel, groups), out_shape=(jax.Sha...  1.58 us

profile of v3, /device:TPU:0, one launch (start us, length us, event | category | flops | bytes accessed | tf_op | source)
XLA Modules:
  0.0 32.2 jit_solution(16880086869212624997)
XLA Ops:
  0.6 30.0 %transport.1 = (f32[4608,128]{1,0:T(8,128)S(1)}, f32[80,128]{1,0:T(8,128)S(1)}, f32[80,128]{1,0:T(8,128)S(1)}) custom-call(f32[4608,128]{1,0:T(8,128)} %bitcast.25, f32[80,128]{1,0:T(8,128)} %bitcast.26, s32[8,128]{1,0:T(8,128)} %bitcast.27, f32[10]{0:T(128)} %rate_hbm.1), custom_call_target="tpu_custom_call" | custom-call | tf_op jit(solution)/shard_map/transport/pallas_call | solution.py:452
  30.6 1.6 %lift.1 = (f32[4608,128]{1,0:T(8,128)}, f32[80,128]{1,0:T(8,128)}) custom-call(f32[4608,128]{1,0:T(8,128)S(1)} %get-tuple-element.7.half_ref, f32[80,128]{1,0:T(8,128)S(1)} %get-tuple-element.8.corr_ref, f32[80,128]{1,0:T(8,128)S(1)} %get-tuple-element.9.mnew_ref), custom_call_target="tpu_custom_call" | custom-call | tf_op jit(solution)/shard_map/lift/pallas_call | solution.py:483

commit v4 on v3

--- a/solution.py
+++ b/solution.py
@@ -124,15 +124,10 @@
 
     lane, row = masks()
     plane = lax.rem(row, ROWS // 2)
-    for copy in small:
-        copy.wait()
-    pore = pore_ref[...].astype(jnp.float32)
-    pore_ext[1] = pore
     edge = jnp.where(positive, 0, ROWS // 2 - 1)
     at_edge = jnp.where(plane == edge, 1.0, 0.0)
     off_edge = 1.0 - at_edge
     acc[...] = jnp.zeros_like(acc)
-    fields = [m_ref[pl.ds(m * ROWS, ROWS), :] for m in range(NMOM)]
 
     def upwind_x(f):
         return jnp.where(positive, pltpu.roll(f, 1, 0), pltpu.roll(f, ROWS - 1, 0))
@@ -251,22 +246,25 @@
                 acc[rows, :] = acc[rows, :] + term
             return carry
 
-        lax.fori_loop(0, HALF, body, 0)
-
-    def prepare(c, carry):
+        lax.fori_loop(0, HALF, body, 0, unroll=3)
+
+    def send_first(c, carry):
         load(c).wait()
         pack_chunk(f_ref, fsend, c)
-        return carry
-
-    lax.fori_loop(0, chunks, prepare, 0)
-
-    pl.semaphore_wait(barrier, nvel + 1)
-
-    def send_first(c, carry):
         send(fsend, frecv, fs_sem, fr_sem, c).start()
         return carry
 
-    lax.fori_loop(0, chunks, send_first, 0)
+    load(0).wait()
+    pack_chunk(f_ref, fsend, 0)
+    pl.semaphore_wait(barrier, nvel + 1)
+    send(fsend, frecv, fs_sem, fr_sem, 0).start()
+    lax.fori_loop(1, chunks, send_first, 0)
+
+    for copy in small:
+        copy.wait()
+    pore = pore_ref[...].astype(jnp.float32)
+    pore_ext[1] = pore
+    fields = [m_ref[pl.ds(m * ROWS, ROWS), :] for m in range(NMOM)]
     pores = edges(pore_ext, pore_ext, ps_sem, pr_sem)
     for copy in pores:
         copy.start()

time: 32.3 us -> 31.8 us (0.985)
  Pallas kernels: 31.5 us -> 31 us
    pallas_call x1, Pallas kernels: 30 us -> 29.5 us  [body(): pl.pallas_call(functools.partial(transport_kernel, nvel, nspace, groups),...]
where the time goes in v4:
time: 31.8 us; the launch traced here: 31.7 us
  Pallas kernels  31 us (97%)
  between operations  0.64 us (2%)
    pallas_call x1, Pallas kernels, body(): pl.pallas_call(functools.partial(transport_kernel, nvel, nspace, groups),...  29.5 us
    pallas_call x1, Pallas kernels, body(): pl.pallas_call(functools.partial(lift_kernel, groups), out_shape=(jax.Sha...  1.58 us

profile of v4, /device:TPU:0, one launch (start us, length us, event | category | flops | bytes accessed | tf_op | source)
XLA Modules:
  0.0 31.7 jit_solution(5439125899086156572)
XLA Ops:
  0.6 29.5 %transport.1 = (f32[4608,128]{1,0:T(8,128)S(1)}, f32[80,128]{1,0:T(8,128)S(1)}, f32[80,128]{1,0:T(8,128)S(1)}) custom-call(f32[4608,128]{1,0:T(8,128)} %bitcast.25, f32[80,128]{1,0:T(8,128)} %bitcast.26, s32[8,128]{1,0:T(8,128)} %bitcast.27, f32[10]{0:T(128)} %rate_hbm.1), custom_call_target="tpu_custom_call" | custom-call | tf_op jit(solution)/shard_map/transport/pallas_call | solution.py:450
  30.1 1.6 %lift.1 = (f32[4608,128]{1,0:T(8,128)}, f32[80,128]{1,0:T(8,128)}) custom-call(f32[4608,128]{1,0:T(8,128)S(1)} %get-tuple-element.7.half_ref, f32[80,128]{1,0:T(8,128)S(1)} %get-tuple-element.8.corr_ref, f32[80,128]{1,0:T(8,128)S(1)} %get-tuple-element.9.mnew_ref), custom_call_target="tpu_custom_call" | custom-call | tf_op jit(solution)/shard_map/lift/pallas_call | solution.py:481
